TPU v7x, 128 devices: a whole 4x4x4 slice. The times are simulated.
128 devices in a mesh: ctx: 32 (over z, x, core), head: 4 (over y).
Axes of the slice: x: 4, y: 4, z: 4, core: 2. Of those that a mesh axis runs over, the one named last changes fastest.
Arguments:
- queries: bfloat16 [131072, 2048], P('ctx', 'head'), may hold values from -6 to 6
- keys: bfloat16 [131072, 2048], P('ctx', 'head'), may hold values from -6 to 6
- values: bfloat16 [131072, 2048], P('ctx', 'head'), may hold values from -6 to 6
- lam_index: int32 [2048], P('ctx'), may hold values from 0 to 15
- level_weights: float32 [16, 16, 12], P(None, 'head'), may hold values from 0.25 to 2
- gate: bfloat16 [131072, 2048], P(('ctx', 'head')), may hold values from -6 to 6
- norm_gain: float32 [2048], replicated, may hold values from 0.25 to 1.75
- out_weight: bfloat16 [2048, 2048], P(None, ('ctx', 'head')), may hold values from -0.125 to 0.125
Outputs:
- output: bfloat16 [131072, 2048], P(('ctx', 'head'))
All inputs are finite; a program needn't handle non-finite values.
Results may differ from a plain program's by a relative error of at most 0.0064.
Values may be sent and summed in bfloat16 or wider, within the bound.
A program may use at most 192 MiB of HBM per device.

v0:
```python
import jax
import jax.numpy as jnp
from jax import lax
from jax.sharding import PartitionSpec as P

DK = 128
D = 2048
SPAN = 64
LEVELS = 12
TABLE = 16


def tree_mix(span_states, coefficient):
    total_count = span_states.shape[0]
    tail_shape = span_states.shape[1:]
    mixed = jnp.zeros_like(span_states)
    partial_value = span_states
    tree_level = 1
    block_width = 1
    while block_width < total_count:
        pair_count = total_count // (2 * block_width)
        paired = partial_value.reshape((pair_count, 2) + tail_shape)
        weight = coefficient[..., tree_level].reshape(
            (pair_count, 2, block_width) + tail_shape[:-2]
        )[:, 1]
        addend = weight[..., None, None] * paired[:, 0][:, None]
        mixed = mixed.reshape((pair_count, 2, block_width) + tail_shape).at[:, 1].add(addend)
        mixed = mixed.reshape((total_count,) + tail_shape)
        partial_value = paired[:, 0] + paired[:, 1]
        tree_level += 1
        block_width *= 2
    return (mixed, partial_value[0])


def local(queries, keys, values, lam_index, level_weights, gate, norm_gain, out_weight):
    tok_rows = queries.shape[0]
    heads_here = level_weights.shape[1]
    span_count = tok_rows // SPAN
    query_blocks = queries.reshape(span_count, SPAN, heads_here, DK)
    key_blocks = keys.reshape(span_count, SPAN, heads_here, DK)
    value_blocks = values.reshape(span_count, SPAN, heads_here, DK)
    level_scale = jnp.exp2(-0.5 * jnp.arange(LEVELS, dtype=jnp.float32)) * DK ** (-0.5)
    weight_table = level_weights.reshape(TABLE, heads_here * LEVELS)
    selector = (lam_index[:, None] == jnp.arange(TABLE, dtype=jnp.int32)[None, :]).astype(
        jnp.float32
    )
    coefficient = jnp.dot(selector, weight_table, precision=lax.Precision.HIGHEST)
    coefficient = coefficient.reshape(span_count, heads_here, LEVELS) * level_scale
    span_states = jnp.einsum(
        "cthk,cthv->chkv", key_blocks, value_blocks, preferred_element_type=jnp.float32
    )
    tree_state, device_total = tree_mix(span_states, coefficient)
    local_levels = span_count.bit_length() - 1
    ctx_bits = lax.axis_size("ctx").bit_length() - 1
    ctx_index = lax.axis_index("ctx")
    bit_order = jnp.arange(ctx_bits, dtype=jnp.int32)
    piece = lax.all_gather(device_total[None], "ctx", axis=0, tiled=True)
    owners = jnp.arange(piece.shape[0], dtype=jnp.int32)
    upper_same = owners[None, :] >> bit_order[:, None] + 1 == ctx_index >> bit_order[:, None] + 1
    lower_half = owners[None, :] >> bit_order[:, None] & 1 == 0
    mine_upper = ctx_index >> bit_order & 1 == 1
    select = (upper_same & lower_half & mine_upper[:, None]).astype(jnp.float32)
    cross_states = jnp.einsum("be,ehkv->bhkv", select, piece, precision=lax.Precision.HIGHEST)
    cross_coef = coefficient[:, :, local_levels + 1 : local_levels + 1 + ctx_bits]
    tree_state = tree_state + jnp.einsum(
        "chb,bhkv->chkv", cross_coef, cross_states, precision=lax.Precision.HIGHEST
    )
    tree_rounded = tree_state.astype(jnp.bfloat16)
    carried = jnp.einsum(
        "cthk,chkv->cthv", query_blocks, tree_rounded, preferred_element_type=jnp.float32
    )
    scores = jnp.einsum(
        "cshk,cthk->chst", query_blocks, key_blocks, preferred_element_type=jnp.float32
    )
    scores = scores * coefficient[:, :, 0][:, :, None, None]
    causal = jnp.arange(SPAN)[:, None] >= jnp.arange(SPAN)[None, :]
    local_weights = jnp.where(causal[None, None], scores, 0.0).astype(jnp.bfloat16)
    local_part = jnp.einsum(
        "chst,cthv->cshv", local_weights, value_blocks, preferred_element_type=jnp.float32
    )
    attention = (local_part + carried).astype(jnp.bfloat16)
    head_count = lax.axis_size("head")
    own_rows = tok_rows // head_count
    attention = attention.reshape(head_count, own_rows, heads_here * DK)
    regrouped = lax.all_to_all(attention, "head", split_axis=0, concat_axis=2, tiled=True).reshape(
        own_rows, D
    )
    gated = regrouped.astype(jnp.float32) * jax.nn.silu(gate.astype(jnp.float32))
    mean_square = jnp.mean(gated * gated, axis=-1, keepdims=True)
    normed = (gated * lax.rsqrt(mean_square + 1e-06) * norm_gain).astype(jnp.bfloat16)
    projected = jnp.dot(
        normed,
        lax.all_gather(out_weight, ("ctx", "head"), axis=1, tiled=True),
        preferred_element_type=jnp.float32,
    )
    return projected.astype(jnp.bfloat16)


def solution(mesh):
    in_specs = (
        P("ctx", "head"),
        P("ctx", "head"),
        P("ctx", "head"),
        P("ctx"),
        P(None, "head", None),
        P(("ctx", "head"), None),
        P(),
        P(None, ("ctx", "head")),
    )
    out_specs = P(("ctx", "head"), None)
    return jax.shard_map(local, mesh=mesh, in_specs=in_specs, out_specs=out_specs, check_vma=False)
```

profile of v0, /device:TPU:0, one launch (start us, length us, event | category | flops | bytes accessed | tf_op | source)
XLA Modules:
  0.0 317.3 jit_solution(7478994671245799801)
XLA Ops:
  8.6 6.9 %reshape.412 = bf16[64,64,4,128]{3,2,1,0:T(4,128)(2,1)} reshape(bf16[4096,512]{1,0:T(8,128)(2,1)} %param.21) | data formatting | bytes 8388608 | tf_op jit(solution)/shard_map/reshape | solution.py:40
  15.5 6.9 %reshape.414 = bf16[64,64,4,128]{3,2,1,0:T(4,128)(2,1)} reshape(bf16[4096,512]{1,0:T(8,128)(2,1)} %param.22) | data formatting | bytes 8388608 | tf_op jit(solution)/shard_map/reshape | solution.py:41
  22.4 11.6 %fusion.25 = f32[64,4,128,128]{3,2,1,0:T(8,128)} fusion(bf16[64,64,4,128]{3,2,1,0:T(4,128)(2,1)} %reshape.414, bf16[64,64,4,128]{3,2,1,0:T(4,128)(2,1)} %reshape.412), kind=kOutput, calls=%fused_computation.43 | convolution fusion | flops 536870912 | bytes 25165824 | tf_op jit(solution)/shard_map/cthk,cthv->chkv/dot_general | solution.py:49
  34.0 9.9 %fusion.9 = (f32[32,1,4,128,128]{4,3,2,0,1:T(8,128)S(1)}, f32[32,1,1,4,128,128]{5,4,3,0,2,1:T(8,128)}) fusion(f32[32,2,4,128,128]{4,3,2,1,0:T(8,128)} %bitcast.103, f32[32,4]{1,0:T(8,128)S(1)} %bitcast.111), kind=kLoop, calls=%fused_computation.17 | loop fusion | flops 4194304 | bytes 33554944 | tf_op jit(solution)/shard_map/add | solution.py:29
  50.1 11.3 %scatter-add.20 = f32[32,2,1,4,128,128]{5,4,3,0,2,1:T(8,128)} pad(f32[32,1,1,4,128,128]{5,4,3,0,2,1:T(8,128)} %get-tuple-element.84, f32[]{:T(128)} %constant.147.clone.1), padding=0_0x1_0x0_0x0_0x0_0x0_0 | pad | bytes 25165828 | tf_op jit(solution)/shard_map/scatter-add | solution.py:27
  61.4 11.8 %copy.135 = f32[16,2,2,4,128,128]{5,4,3,2,1,0:T(8,128)} copy(f32[16,2,2,4,128,128]{5,4,3,1,0,2:T(8,128)} %bitcast.104) | data formatting | bytes 33554432 | tf_op jit(solution)/shard_map/reshape;reshape | solution.py:27
  73.9 7.8 %fusion.10 = f32[16,2,2,4,128,128]{5,4,3,2,1,0:T(8,128)} fusion(f32[16,2,2,4,128,128]{5,4,3,2,1,0:T(8,128)} %copy.135, f32[16,4,128,128]{3,2,1,0:T(8,128)} %get-tuple-element.86, f32[16,2,4]{2,1,0:T(2,128)S(1)} %slice_bitcast_fusion.9), kind=kLoop, calls=%fused_computation.19 | loop fusion | flops 4194304 | bytes 20972032 | tf_op jit(solution)/shard_map/scatter-add | solution.py:27
  81.7 6.6 %fusion.8 = f32[8,2,4,4,128,128]{5,4,3,2,1,0:T(8,128)} fusion(f32[8,2,4,4,128,128]{5,4,3,2,1,0:T(8,128)} %bitcast.98, f32[8,4,128,128]{3,2,1,0:T(8,128)S(1)} %get-tuple-element.88, f32[8,4,4]{2,1,0:T(4,128)S(1)} %copy.137), kind=kLoop, calls=%fused_computation.15 | loop fusion | flops 4194304 | bytes 18874880 | tf_op jit(solution)/shard_map/scatter-add | solution.py:27
  88.3 7.8 %fusion.7 = f32[4,2,8,4,128,128]{5,4,3,2,1,0:T(8,128)} fusion(f32[4,2,8,4,128,128]{5,4,3,2,1,0:T(8,128)} %bitcast.99, f32[4,4,128,128]{3,2,1,0:T(8,128)S(1)} %get-tuple-element.90, f32[4,8,4]{2,1,0:T(8,128)S(1)} %copy.139), kind=kLoop, calls=%fused_computation.13 | loop fusion | flops 4194304 | bytes 17826304 | tf_op jit(solution)/shard_map/scatter-add | solution.py:27
  96.1 18.0 %copy.144 = f32[2,2,16,4,128,128]{5,2,1,0,4,3:T(8,128)} copy(f32[2,2,16,4,128,128]{5,4,3,2,1,0:T(8,128)} %bitcast.100) | data formatting | bytes 33554432 | tf_op jit(solution)/shard_map/reshape;reshape | solution.py:27
  114.7 6.9 %reshape.411 = bf16[64,64,4,128]{3,2,1,0:T(4,128)(2,1)} reshape(bf16[4096,512]{1,0:T(8,128)(2,1)} %param.20) | data formatting | bytes 8388608 | tf_op jit(solution)/shard_map/reshape | solution.py:39
  121.7 8.2 %fusion.6 = f32[2,2,16,4,128,128]{5,2,1,0,4,3:T(8,128)} fusion(f32[2,2,16,4,128,128]{5,2,1,0,4,3:T(8,128)} %copy.144, f32[2,4,128,128]{3,0,2,1:T(2,128)S(1)} %copy.143, f32[2,16,4]{1,0,2:T(2,128)S(1)} %copy.142), kind=kLoop, calls=%fused_computation.11 | loop fusion | flops 4194304 | bytes 17302016 | tf_op jit(solution)/shard_map/scatter-add | solution.py:27
  129.9 8.1 %fusion.5 = f32[1,2,32,4,128,128]{5,2,1,4,3,0:T(8,128)} fusion(f32[1,2,32,4,128,128]{5,2,1,4,3,0:T(8,128)} %bitcast.101, f32[4,128,128]{2,1,0:T(8,128)S(1)} %get-tuple-element.94, f32[32,4]{0,1:T(4,128)S(1)} %bitcast.116), kind=kLoop, calls=%fused_computation.9 | loop fusion | flops 4194304 | bytes 17039872 | tf_op jit(solution)/shard_map/scatter-add | solution.py:27
  138.0 10.8 %fusion.12 = f32[5,4,128,128]{3,0,2,1:T(8,128)S(1)} fusion(f32[32,1,4,128,128]{4,3,2,1,0:T(8,128)} %all-gather.6.cloned.1.call-done, s32[5]{0:T(128)S(1)} %get-tuple-element.99, s32[5]{0:T(128)S(1)} %get-tuple-element.98, pred[5]{0:T(512)(128)(4,1)S(1)} %and_compare_fusion.1), kind=kOutput, calls=%fused_computation.24 | convolution fusion | flops 125830240 | bytes 9699373 | tf_op jit(solution)/shard_map/be,ehkv->bhkv/dot_general | solution.py:63
  148.8 16.8 %fusion = bf16[64,4,128,128]{3,0,2,1:T(8,128)(2,1)S(1)} fusion(f32[64,4,128,128]{3,0,2,1:T(8,128)} %bitcast.102, f32[5,4,128,128]{3,0,2,1:T(8,128)S(1)} %fusion.12, f32[64,4,12]{0,2,1:T(8,128)S(1)} %convolution_multiply_fusion), kind=kOutput, calls=%fused_computation.1 | convolution fusion | flops 260046848 | bytes 27279360 | tf_op jit(solution)/shard_map/chb,bhkv->chkv/dot_general | solution.py:65
  165.6 20.1 %fusion.14 = f32[64,4,128,64]{2,3,1,0:T(8,128)} fusion(bf16[64,4,128,128]{3,0,2,1:T(8,128)(2,1)S(1)} %fusion, bf16[64,64,4,128]{3,2,1,0:T(4,128)(2,1)S(1)} %copy-done), kind=kOutput, calls=%fused_computation.26 | convolution fusion | flops 536870912 | bytes 20971520 | tf_op jit(solution)/shard_map/cthk,chkv->cthv/dot_general | solution.py:69
  185.7 10.7 %fusion.11 = bf16[64,64,4,128]{3,1,2,0:T(8,128)(2,1)} fusion(f32[64,4,128,64]{2,3,1,0:T(8,128)} %fusion.14, bf16[64,64,4,128]{3,2,1,0:T(4,128)(2,1)} %reshape.414, f32[64,4]{1,0:T(8,128)S(1)} %copy.122, pred[64,64]{1,0:T(8,128)(4,1)S(1)} %iota_compare_fusion, bf16[64,64,4,128]{3,2,1,0:T(4,128)(2,1)} %reshape.412, bf16[64,64,4,128]{3,2,1,0:T(4,128)(2,1)} %reshape.411), kind=kOutput, calls=%fused_computation.23 | convolution fusion | flops 544210944 | bytes 25170944 | tf_op jit(solution)/shard_map/chst,cthv->cshv/dot_general | solution.py:78
  196.4 12.5 %copy.149 = bf16[64,64,4,128]{3,2,1,0:T(4,128)(2,1)} copy(bf16[64,64,4,128]{3,1,2,0:T(8,128)(2,1)} %fusion.11) | data formatting | bytes 8388608 | tf_op jit(solution)/shard_map/convert_element_type | solution.py:81
  209.0 7.2 %reshape.417 = bf16[4,1024,512]{2,1,0:T(8,128)(2,1)} reshape(bf16[64,64,4,128]{3,2,1,0:T(4,128)(2,1)} %copy.149) | data formatting | bytes 8388608 | tf_op jit(solution)/shard_map/reshape | solution.py:84
  227.9 42.9 %all-to-all-done = bf16[4,1024,512]{2,1,0:T(8,128)(2,1)} async-done(((bf16[4,1024,512]{2,1,0:T(8,128)(2,1)}), bf16[4,1024,512]{2,1,0:T(8,128)(2,1)}, u32[]{:S(2)}, u32[]{:S(2)}) %all-to-all-start) | async-done | bytes 4194336 | tf_op jit(solution)/shard_map/all_to_all | solution.py:85
  270.9 6.6 %convert_bitcast_fusion = f32[1,1024,4,512]{3,1,2,0:T(8,128)} fusion(bf16[4,1024,512]{2,1,0:T(8,128)(2,1)} %all-to-all-done), kind=kLoop, calls=%fused_computation.21 | loop fusion | flops 2097152 | bytes 12582912 | tf_op jit(solution)/shard_map/convert_element_type | solution.py:88
  277.5 8.7 %copy.150 = f32[1,1024,4,512]{1,3,2,0:T(8,128)} copy(f32[1,1024,4,512]{3,1,2,0:T(8,128)} %convert_bitcast_fusion) | data formatting | bytes 16777216 | tf_op jit(solution)/shard_map/convert_element_type | solution.py:88
  286.2 8.2 %multiply_reduce_fusion = (f32[1024]{0:T(1024)S(1)}, f32[1024,2048]{0,1:T(8,128)}) fusion(bf16[1024,2048]{0,1:T(8,128)(2,1)} %copy.151, f32[1,1024,4,512]{1,3,2,0:T(8,128)} %copy.150), kind=kLoop, calls=%fused_computation.30 | loop fusion | flops 16776192 | bytes 20975616 | tf_op jit(solution)/shard_map/reduce_sum | solution.py:89
  294.4 15.9 %fusion.24 = bf16[1024,2048]{1,0:T(8,128)(2,1)} fusion(bf16[2048,2048]{0,1:T(8,128)(2,1)} %all-gather.4.cloned.1.call-done, f32[1024,2048]{0,1:T(8,128)} %get-tuple-element.82, f32[2048]{0:T(1024)S(1)} %copy-done.2, f32[1024]{0:T(1024)S(1)} %add_rsqrt_fusion), kind=kOutput, calls=%fused_computation.42 | convolution fusion | flops 8598323200 | bytes 20983808 | tf_op jit(solution)/shard_map/dot_general | solution.py:91
  (48 shorter events, 21.3 us)
Async XLA Ops:
  6.5 131.5 %all-gather.6.cloned.1.call-start = ((), (), s32[]{:S(2)}) async-start(), calls=%async_computation.2 | async-start | bytes 8650752 | tf_op jit(solution)/shard_map/all_gather | solution.py:57
  49.4 245.0 %all-gather.4.cloned.1.call-start = ((), (), s32[]{:S(2)}) async-start(), calls=%async_computation.1 | async-start | bytes 8454144 | tf_op jit(solution)/shard_map/all_gather | solution.py:93
  96.1 18.0 %copy-start.1 = (f32[2,4,128,128]{3,2,1,0:T(8,128)S(1)}, f32[2,4,128,128]{3,2,1,0:T(8,128)}, u32[]{:S(2)}) copy-start(f32[2,4,128,128]{3,2,1,0:T(8,128)} %get-tuple-element.92) | copy-start | bytes 1572868
  148.8 16.8 %copy-start = (bf16[64,64,4,128]{3,2,1,0:T(4,128)(2,1)S(1)}, bf16[64,64,4,128]{3,2,1,0:T(4,128)(2,1)}, u32[]{:S(2)}) copy-start(bf16[64,64,4,128]{3,2,1,0:T(4,128)(2,1)} %reshape.411) | copy-start | bytes 12582916
  216.2 54.7 %all-to-all-start = ((bf16[4,1024,512]{2,1,0:T(8,128)(2,1)}), bf16[4,1024,512]{2,1,0:T(8,128)(2,1)}, u32[]{:S(2)}, u32[]{:S(2)}) async-start(bf16[4,1024,512]{2,1,0:T(8,128)(2,1)} %reshape.417), calls=%async_computation | async-start | bytes 8388608 | tf_op jit(solution)/shard_map/all_to_all | solution.py:85
  286.2 8.2 %copy-start.2 = (f32[2048]{0:T(1024)S(1)}, f32[2048]{0:T(1024)}, u32[]{:S(2)}) copy-start(f32[2048]{0:T(1024)} %param.26) | copy-start | bytes 24580
Sparse Core Ops, SparseCore 0:
  49.5 55.4 all-gather.5
  108.2 69.6 all-gather.3
where the time goes:
time: 323 us; the launch traced here: 317 us
  local copies, waits for them, and re-layouts  99.1 us (31%)
  matrix products  86.7 us (27%)
  other arithmetic  68.6 us (21%)
  waiting for transfers between devices  43.1 us (13%)
  between operations  13.7 us (4%)
  starting transfers between devices  5.94 us (2%)
    all_to_all x1, waiting for transfers between devices, local(): lax.all_to_all(attention, 'head', split_axis=0, concat_axis=2, tiled=True)  42.9 us
    scatter-add x5, other arithmetic, tree_mix(): mixed.reshape((pair_count, 2, block_width) + tail_shape).at[:, 1]  38.5 us
    another operation x2, local copies, waits for them, and re-layouts, tree_mix(): mixed.reshape((pair_count, 2, block_width) + tail_shape).at[:, 1]  29.8 us
    dot_general x1, matrix products, local(): jnp.einsum('cthk,chkv->cthv', query_blocks, tree_rounded, preferred_eleme...  20.1 us
    dot_general x1, matrix products, local(): jnp.einsum('chb,bhkv->chkv', cross_coef, cross_states, precision=lax.Prec...  16.8 us
    dot_general x1, matrix products, local(): jnp.dot(normed, lax.all_gather(out_weight, ('ctx', 'head'), axis=1, tiled...  15.9 us
    add x6, other arithmetic, tree_mix(): partial_value = paired[:, 0] + paired[:, 1]  15.3 us
    convert_element_type x1, local copies, waits for them, and re-layouts, local(): attention = (local_part + carried).astype(jnp.bfloat16)  12.5 us
  transfers between devices with their start and end apart: 3, of which 1 were waited for; matrix products, arithmetic and copies ran while one was open for 62% of the time, Pallas kernels for 0%

commit v1 on v0

v1 whole, which is shorter than its diff:
```python
import functools

import jax
import jax.numpy as jnp
from jax import lax
from jax.experimental import pallas as pl
from jax.experimental.pallas import tpu as pltpu
from jax.sharding import PartitionSpec as P

DK = 128
SPAN = 64
LEVELS = 12
GROUP = 4
GR = GROUP * SPAN
SCALE = [2.0 ** (-0.5 * l) * DK**-0.5 for l in range(LEVELS)]
MESH = pl.DeviceIdType.MESH
F32 = jnp.float32
BF16 = jnp.bfloat16
NT = (((1,), (1,)), ((), ()))
TN = (((0,), (0,)), ((), ()))


def partner(i, m):
    if m == 1:
        return i + 1 - 2 * lax.rem(i, 2)
    if m == 2:
        return i + 2 - 4 * (i // 2)
    return 3 - i


def flip(i):
    return i + 1 - 2 * lax.rem(i, 2)


def kernel(
    lam, lw, q_hbm, k_hbm, v_hbm, gate_hbm, gain, w_hbm, out_hbm,
    qv, kv, vv, gv, att, wv, ov, nrm, gst, p2, p4, p8, tot, tsib, cown, csend, crecv, rsend, rrecv, xfull,
    local_sem, ssem, rsem,
):
    ctx = lax.axis_index("ctx")
    y = lax.axis_index("head")
    core = lax.rem(ctx, 2)
    x = lax.rem(ctx // 2, 4)
    z = ctx // 8

    def dev(zz, xx, cc, yy):
        return (zz * 8 + xx * 2 + cc, yy)

    sib = dev(z, x, 1 - core, y)
    xp = {m: dev(z, partner(x, m), core, y) for m in (1, 2, 3)}
    zp = {m: dev(partner(z, m), x, core, y) for m in (1, 2, 3)}
    yp = {m: dev(z, x, core, partner(y, m)) for m in (1, 2, 3)}

    counter = [0]

    def remote(src, dst, device):
        i = counter[0]
        counter[0] += 1
        return pltpu.make_async_remote_copy(
            src_ref=src, dst_ref=dst, send_sem=ssem.at[i], recv_sem=rsem.at[i],
            device_id=device, device_id_type=MESH,
        )

    lcount = [0]

    def local(src, dst):
        i = lcount[0]
        lcount[0] += 1
        return pltpu.make_async_copy(src, dst, local_sem.at[i])

    everything = []

    def go(copies):
        for c in copies:
            c.start()
        everything.extend(copies)
        return copies

    def arrived(copies):
        for c in copies:
            c.wait_recv()

    w_load = local(w_hbm, wv.at[z, x, core, pl.ds(pl.multiple_of(y * 16, 16), 16)])
    w_load.start()
    kv_loads = []
    for c in range(4):
        rows = pl.ds(c * 1024, 1024)
        pair = (local(k_hbm.at[rows], kv.at[rows]), local(v_hbm.at[rows], vv.at[rows]))
        for cp in pair:
            cp.start()
        kv_loads.append(pair)
    q_load = local(q_hbm, qv)
    q_load.start()
    g_load = local(gate_hbm, gv)
    g_load.start()

    barrier = pltpu.get_barrier_semaphore()
    friends = [sib] + [d[m] for d in (xp, zp, yp) for m in (1, 2, 3)]
    for f in friends:
        pl.semaphore_signal(barrier, inc=1, device_id=f, device_id_type=MESH)
    pl.semaphore_wait(barrier, len(friends))

    w_load.wait()
    mine = wv.at[z, x, core, pl.ds(pl.multiple_of(y * 16, 16), 16)]
    wy = go([remote(mine, mine, yp[m]) for m in (1, 2, 3)])

    w1 = None
    for c in range(4):
        for cp in kv_loads[c]:
            cp.wait()

        def states(i, carry):
            g = c * 4 + i
            rows = pl.ds(pl.multiple_of(g * GR, GR), GR)
            for h in range(4):
                cols = slice(h * DK, (h + 1) * DK)
                gst[h, g] = lax.dot_general(kv[rows, cols], vv[rows, cols], TN, preferred_element_type=F32)
            return carry

        lax.fori_loop(0, 4, states, 0)
        for h in range(4):
            p2[h, 2 * c] = gst[h, 4 * c] + gst[h, 4 * c + 1]
            p2[h, 2 * c + 1] = gst[h, 4 * c + 2] + gst[h, 4 * c + 3]
            p4[h, c] = p2[h, 2 * c] + p2[h, 2 * c + 1]
        if c == 1:
            arrived(wy)
            a_own = wv.at[z, x, core, pl.ds(0, 32)]
            b_own = wv.at[z, x, core, pl.ds(32, 32)]
            w1 = go([remote(a_own, a_own, xp[m]) for m in (1, 2, 3)] + [remote(b_own, b_own, zp[m]) for m in (1, 2, 3)])
    for h in range(4):
        p8[h, 0] = p4[h, 0] + p4[h, 1]
        p8[h, 1] = p4[h, 2] + p4[h, 3]
        tot[h] = p8[h, 0] + p8[h, 1]

    half = pl.ds(core * 2, 2)
    t_copy = go([remote(tot, tsib, sib)])
    arrived(t_copy)
    cown[...] = tot[half] + tsib[half]
    csend[...] = cown[...].astype(BF16)
    c_copy = go([remote(csend, crecv.at[m - 1], xp[m]) for m in (1, 2, 3)])
    arrived(c_copy)
    rsend[...] = (
        (cown[...] + crecv[0].astype(F32)) + (crecv[1].astype(F32) + crecv[2].astype(F32))
    ).astype(BF16)
    r_copy = go([remote(rsend, rrecv.at[m - 1], zp[m]) for m in (1, 2, 3)])
    xfull[0, half] = crecv[0].astype(F32)
    xfull[1, half] = crecv[1].astype(F32) + crecv[2].astype(F32)
    x12 = xfull.at[pl.ds(0, 2), half]
    x12_copy = go([remote(x12, x12, sib)])
    arrived(w1)
    w2b_src = wv.at[:, x, core, pl.ds(32, 32)]
    w2b = go([remote(w2b_src, w2b_src, xp[m]) for m in (1, 2, 3)])
    arrived(r_copy)
    xfull[2, half] = rrecv[0].astype(F32)
    xfull[3, half] = rrecv[1].astype(F32) + rrecv[2].astype(F32)
    x34 = xfull.at[pl.ds(2, 2), half]
    x34_copy = go([remote(x34, x34, sib)])
    w2a_src = wv.at[z, :, core, pl.ds(0, 32)]
    w2a = go([remote(w2a_src, w2a_src, zp[m]) for m in (1, 2, 3)])
    arrived(x12_copy)
    arrived(x34_copy)
    fwd = go([remote(s, s, sib) for s in (w2a_src, w2b_src)])
    q_load.wait()

    bits = [core, lax.rem(x, 2), x // 2, lax.rem(z, 2), z // 2]
    cross_bit = [b.astype(F32) for b in bits]
    lane = lax.broadcasted_iota(jnp.int32, (SPAN, DK), 1)
    row = lax.broadcasted_iota(jnp.int32, (SPAN, DK), 0)
    low = lane <= row
    high = lane <= row + SPAN
    left = lane < SPAN

    def attend(g, put):
        rows = pl.ds(pl.multiple_of(g * GR, GR), GR)
        g2, g4, g8 = g // 2, g // 4, g // 8
        own_bit = [lax.rem(b, 2).astype(F32) for b in (g, g2, g4, g8)]
        s1, s2, s4, s8 = flip(g), flip(g2), flip(g4), flip(g8)
        for h in range(4):
            cols = slice(h * DK, (h + 1) * DK)
            qg, kg, vg = qv[rows, cols], kv[rows, cols], vv[rows, cols]
            s = lax.dot_general(qg, kg, NT, preferred_element_type=F32)
            near, far = [], []
            for p in range(GROUP):
                tab = lam[g * GROUP + p]
                w = [lw[l, h, tab] * SCALE[l] for l in range(3)]
                far.append(
                    [lw[3 + i, h, tab] * (SCALE[3 + i] * own_bit[i]) for i in range(4)]
                    + [lw[7 + i, h, tab] * (SCALE[7 + i] * cross_bit[i]) for i in range(5)]
                )
                sp = s[p * SPAN : (p + 1) * SPAN]
                diag = sp[:, (p // 2) * DK : (p // 2 + 1) * DK]
                if p % 2 == 0:
                    diag = jnp.where(low, diag * w[0], 0.0)
                else:
                    diag = jnp.where(high, diag * jnp.where(left, w[1], w[0]), 0.0)
                near.append(
                    diag.astype(BF16)
                    if p < 2
                    else jnp.concatenate([(sp[:, :DK] * w[2]).astype(BF16), diag.astype(BF16)], axis=1)
                )
            part = [
                jnp.dot(jnp.concatenate(near[:2], axis=0), vg[: 2 * SPAN], preferred_element_type=F32),
                jnp.dot(jnp.concatenate(near[2:], axis=0), vg, preferred_element_type=F32),
            ]
            mixed = [[] for _ in range(GROUP)]
            for r in range(0, DK, 32):
                tile = slice(r, r + 32)
                terms = [
                    gst[h, s1, tile, :], p2[h, s2, tile, :], p4[h, s4, tile, :], p8[h, s8, tile, :], tsib[h, tile, :],
                    xfull[0, h, tile, :], xfull[1, h, tile, :], xfull[2, h, tile, :], xfull[3, h, tile, :],
                ]
                for p in range(GROUP):
                    acc = terms[0] * far[p][0]
                    for term, weight in zip(terms[1:], far[p][1:]):
                        acc = acc + term * weight
                    mixed[p].append(acc.astype(BF16))
            res = []
            for p in range(GROUP):
                carried = jnp.dot(
                    qg[p * SPAN : (p + 1) * SPAN], jnp.concatenate(mixed[p], axis=0), preferred_element_type=F32
                )
                res.append((part[p // 2][(p % 2) * SPAN : (p % 2 + 1) * SPAN] + carried).astype(BF16))
            put(cols, rows, jnp.concatenate(res, axis=0))

    att_copies = []
    for j in range(4):
        def to_send(cols, rows, value):
            qv[rows, cols] = value

        def keep(cols, rows, value, j=j):
            att[y, pl.ds(j * GR, GR), cols] = value

        batch = []
        for m in (2, 1, 3):
            g = partner(y, m) * 4 + j
            attend(g, to_send)
            batch += go([
                remote(qv.at[pl.ds(pl.multiple_of(g * GR, GR), GR)], att.at[y, pl.ds(j * GR, GR)], yp[m])
            ])
        att_copies.append(batch)
        attend(y * 4 + j, keep)

    arrived(w2a)
    arrived(w2b)
    for m in (1, 2, 3):
        a = wv.at[partner(z, m), :, core, pl.ds(0, 32)]
        b = wv.at[:, partner(x, m), core, pl.ds(32, 32)]
        fwd += go([remote(a, a, sib), remote(b, b, sib)])
    arrived(fwd)
    g_load.wait()

    stores = []
    for j in range(4):
        arrived(att_copies[j])

        def normalize(i, carry, j=j):
            rows = pl.ds(pl.multiple_of(j * GR + i * 16, 16), 16)
            a = jnp.concatenate([att[s, rows, :] for s in range(4)], axis=1).astype(F32)
            gt = gv[rows, :].astype(F32)
            gated = a * (gt / (1.0 + jnp.exp(-gt)))
            mean = jnp.mean(gated * gated, axis=1, keepdims=True)
            nrm[pl.ds(pl.multiple_of(i * 16, 16), 16), :] = (
                gated * lax.rsqrt(mean + 1e-6) * gain[...]
            ).astype(BF16)
            return carry

        lax.fori_loop(0, GR // 16, normalize, 0)
        for n in range(4):
            w = wv[n].reshape(512, 2048)
            ov[pl.ds(j * GR, GR), n * 512 : (n + 1) * 512] = lax.dot_general(
                nrm[...], w, NT, preferred_element_type=F32
            ).astype(BF16)
        st = local(ov.at[pl.ds(j * GR, GR)], out_hbm.at[pl.ds(j * GR, GR)])
        st.start()
        stores.append(st)

    for st in stores:
        st.wait()
    for c in everything:
        c.wait_send()


def local_step(queries, keys, values, lam_index, level_weights, gate, norm_gain, out_weight):
    any_spec = pl.BlockSpec(memory_space=pl.ANY)
    smem = pl.BlockSpec(memory_space=pltpu.SMEM)
    vmem = pl.BlockSpec(memory_space=pltpu.VMEM)
    return pl.pallas_call(
        kernel,
        out_shape=jax.ShapeDtypeStruct((1024, 2048), BF16),
        in_specs=[smem, smem, any_spec, any_spec, any_spec, any_spec, vmem, any_spec],
        out_specs=any_spec,
        scratch_shapes=[
            pltpu.VMEM((4096, 512), BF16),
            pltpu.VMEM((4096, 512), BF16),
            pltpu.VMEM((4096, 512), BF16),
            pltpu.VMEM((1024, 2048), BF16),
            pltpu.VMEM((4, 1024, 512), BF16),
            pltpu.VMEM((4, 4, 2, 64, 2048), BF16),
            pltpu.VMEM((1024, 2048), BF16),
            pltpu.VMEM((GR, 2048), BF16),
            pltpu.VMEM((4, 16, DK, DK), F32),
            pltpu.VMEM((4, 8, DK, DK), F32),
            pltpu.VMEM((4, 4, DK, DK), F32),
            pltpu.VMEM((4, 2, DK, DK), F32),
            pltpu.VMEM((4, DK, DK), F32),
            pltpu.VMEM((4, DK, DK), F32),
            pltpu.VMEM((2, DK, DK), F32),
            pltpu.VMEM((2, DK, DK), BF16),
            pltpu.VMEM((3, 2, DK, DK), BF16),
            pltpu.VMEM((2, DK, DK), BF16),
            pltpu.VMEM((3, 2, DK, DK), BF16),
            pltpu.VMEM((4, 4, DK, DK), F32),
            pltpu.SemaphoreType.DMA((16,)),
            pltpu.SemaphoreType.DMA((48,)),
            pltpu.SemaphoreType.DMA((48,)),
        ],
        compiler_params=pltpu.CompilerParams(
            collective_id=0, has_side_effects=True, vmem_limit_bytes=58 * 1024 * 1024
        ),
    )(
        lam_index, jnp.transpose(level_weights, (2, 1, 0)), queries, keys, values, gate,
        norm_gain.reshape(1, 2048), jnp.transpose(out_weight),
    )


def solution(mesh):
    in_specs = (
        P("ctx", "head"),
        P("ctx", "head"),
        P("ctx", "head"),
        P("ctx"),
        P(None, "head", None),
        P(("ctx", "head"), None),
        P(),
        P(None, ("ctx", "head")),
    )
    out_specs = P(("ctx", "head"), None)
    return jax.shard_map(local_step, mesh=mesh, in_specs=in_specs, out_specs=out_specs, check_vma=False)
```

time: 323 us -> 89.9 us (0.28); the launches traced: 317 us -> 88.7 us
  local copies, waits for them, and re-layouts: 99.1 us -> 4.79 us
  matrix products: 86.7 us -> 0 us
  Pallas kernels: 0 us -> 83.9 us
  other arithmetic: 68.6 us -> 0 us
  waiting for transfers between devices: 43.1 us -> 0 us
  between operations: 13.7 us -> 0.01 us
  starting transfers between devices: 5.94 us -> 0 us
    dot_general x7 -> x0, matrix products: 86.7 us -> none  [the longest x1 20.1 us: local(): jnp.einsum('cthk,chkv->cthv', query_blocks, tree_rounded, preferred_eleme...]
    pallas_call x0 -> x1, Pallas kernels: none -> 83.9 us  [local_step(): pl.pallas_call(kernel, out_shape=jax.ShapeDtypeStruct((1024, 2048), BF16)...]
    all_to_all x1 -> x0, waiting for transfers between devices: 42.9 us -> none  [local(): lax.all_to_all(attention, 'head', split_axis=0, concat_axis=2, tiled=True)]
    scatter-add x5 -> x0, other arithmetic: 38.5 us -> none  [tree_mix(): mixed.reshape((pair_count, 2, block_width) + tail_shape).at[:, 1]]
    another operation x6 -> x0, local copies, waits for them, and re-layouts: 30.2 us -> none  [the longest x2 29.8 us: tree_mix(): mixed.reshape((pair_count, 2, block_width) + tail_shape).at[:, 1]]
    reshape x5 -> x0, local copies, waits for them, and re-layouts: 28 us -> none  [the longest x1 7.19 us: local(): attention = attention.reshape(head_count, own_rows, heads_here * DK)]
    convert_element_type x2 -> x0, local copies, waits for them, and re-layouts: 21.2 us -> none  [the longest x1 12.5 us: local(): attention = (local_part + carried).astype(jnp.bfloat16)]
    add x7 -> x0, other arithmetic: 15.3 us -> none  [the longest x6 15.3 us: tree_mix(): partial_value = paired[:, 0] + paired[:, 1]]
  transfers between devices with their start and end apart: 3 -> 0, of which waited for: 1 -> 0; matrix products, arithmetic and copies ran while one was open for 62% -> 0% of each run, Pallas kernels for 0% -> 0%
where the time goes in v1:
time: 89.9 us; the launch traced here: 88.7 us
  Pallas kernels  83.9 us (93%)
  local copies, waits for them, and re-layouts  4.79 us (5%)
    pallas_call x1, Pallas kernels, local_step(): pl.pallas_call(kernel, out_shape=jax.ShapeDtypeStruct((1024, 2048), BF16)...  83.9 us
    unnamed x1, local copies, waits for them, and re-layouts  4.79 us

profile of v1, /device:TPU:0, one launch (start us, length us, event | category | flops | bytes accessed | tf_op | source)
XLA Modules:
  0.0 88.7 jit_solution(5968287251191975485)
XLA Ops:
  0.0 83.9 %shard_map.82 = bf16[1024,2048]{1,0:T(8,128)(2,1)} custom-call(s32[64]{0:T(128)} %lam.1, f32[12,4,16]{2,1,0:T(4,128)} %bitcast.4, bf16[4096,512]{1,0:T(8,128)(2,1)} %q_hbm.1, bf16[4096,512]{1,0:T(8,128)(2,1)} %k_hbm.1, bf16[4096,512]{1,0:T(8,128)(2,1)} %v_hbm.1, bf16[1024,2048]{1,0:T(8,128)(2,1)} %gate_hbm.1, f32[1,2048]{1,0:T(1,128)} %bitcast.5, ...), custom_call_target="tpu_custom_call" | custom-call | tf_op jit(solution)/shard_map/pallas_call | solution.py:287
  83.9 4.8 %copy.10 = bf16[1024,2048]{1,0:T(8,128)(2,1)} copy(bf16[1024,2048]{1,0:T(8,128)(2,1)} %shard_map.82) | data formatting | bytes 8388608

commit v2 on v1

--- a/solution.py
+++ b/solution.py
@@ -15,6 +15,7 @@
 SCALE = [2.0 ** (-0.5 * l) * DK**-0.5 for l in range(LEVELS)]
 MESH = pl.DeviceIdType.MESH
 F32 = jnp.float32
+UNROLL = True
 BF16 = jnp.bfloat16
 NT = (((1,), (1,)), ((), ()))
 TN = (((0,), (0,)), ((), ()))
@@ -33,9 +34,9 @@
 
 
 def kernel(
-    lam, lw, q_hbm, k_hbm, v_hbm, gate_hbm, gain, w_hbm, out_hbm,
-    qv, kv, vv, gv, att, wv, ov, nrm, gst, p2, p4, p8, tot, tsib, cown, csend, crecv, rsend, rrecv, xfull,
-    local_sem, ssem, rsem,
+    lam, lw, q_hbm, k_hbm, v_hbm, gate_hbm, gain, w_hbm, ov, nrm, wv,
+    qv, kv, vv, gv, att, gst, p2, p4, p8, tot, tsib, cown, csend, crecv, rsend, rrecv, xfull,
+    local_sem, ssem, rsem, att_send, att_recv,
 ):
     ctx = lax.axis_index("ctx")
     y = lax.axis_index("head")
@@ -98,13 +99,7 @@
     friends = [sib] + [d[m] for d in (xp, zp, yp) for m in (1, 2, 3)]
     for f in friends:
         pl.semaphore_signal(barrier, inc=1, device_id=f, device_id_type=MESH)
-    pl.semaphore_wait(barrier, len(friends))
-
-    w_load.wait()
-    mine = wv.at[z, x, core, pl.ds(pl.multiple_of(y * 16, 16), 16)]
-    wy = go([remote(mine, mine, yp[m]) for m in (1, 2, 3)])
-
-    w1 = None
+
     for c in range(4):
         for cp in kv_loads[c]:
             cp.wait()
@@ -117,49 +112,61 @@
                 gst[h, g] = lax.dot_general(kv[rows, cols], vv[rows, cols], TN, preferred_element_type=F32)
             return carry
 
-        lax.fori_loop(0, 4, states, 0)
+        lax.fori_loop(0, 4, states, 0, unroll=UNROLL)
         for h in range(4):
             p2[h, 2 * c] = gst[h, 4 * c] + gst[h, 4 * c + 1]
             p2[h, 2 * c + 1] = gst[h, 4 * c + 2] + gst[h, 4 * c + 3]
             p4[h, c] = p2[h, 2 * c] + p2[h, 2 * c + 1]
-        if c == 1:
-            arrived(wy)
-            a_own = wv.at[z, x, core, pl.ds(0, 32)]
-            b_own = wv.at[z, x, core, pl.ds(32, 32)]
-            w1 = go([remote(a_own, a_own, xp[m]) for m in (1, 2, 3)] + [remote(b_own, b_own, zp[m]) for m in (1, 2, 3)])
     for h in range(4):
         p8[h, 0] = p4[h, 0] + p4[h, 1]
         p8[h, 1] = p4[h, 2] + p4[h, 3]
         tot[h] = p8[h, 0] + p8[h, 1]
 
-    half = pl.ds(core * 2, 2)
-    t_copy = go([remote(tot, tsib, sib)])
-    arrived(t_copy)
-    cown[...] = tot[half] + tsib[half]
-    csend[...] = cown[...].astype(BF16)
-    c_copy = go([remote(csend, crecv.at[m - 1], xp[m]) for m in (1, 2, 3)])
-    arrived(c_copy)
-    rsend[...] = (
-        (cown[...] + crecv[0].astype(F32)) + (crecv[1].astype(F32) + crecv[2].astype(F32))
-    ).astype(BF16)
-    r_copy = go([remote(rsend, rrecv.at[m - 1], zp[m]) for m in (1, 2, 3)])
-    xfull[0, half] = crecv[0].astype(F32)
-    xfull[1, half] = crecv[1].astype(F32) + crecv[2].astype(F32)
-    x12 = xfull.at[pl.ds(0, 2), half]
-    x12_copy = go([remote(x12, x12, sib)])
-    arrived(w1)
+    w_load.wait()
+    pl.semaphore_wait(barrier, len(friends))
+    mine_h = [2 * core, 2 * core + 1]
+    sib_h = [2 * (1 - core), 2 * (1 - core) + 1]
+    t_copy = [go([remote(tot.at[h], tsib.at[h], sib)]) for h in sib_h]
+    mine = wv.at[z, x, core, pl.ds(pl.multiple_of(y * 16, 16), 16)]
+    wy = go([remote(mine, mine, yp[m]) for m in (1, 2, 3)])
+    t_copy += [go([remote(tot.at[h], tsib.at[h], sib)]) for h in mine_h]
+    c_copy = []
+    for i in range(2):
+        arrived(t_copy[i])
+        cown[i] = tot[mine_h[i]] + tsib[mine_h[i]]
+        csend[i] = cown[i].astype(BF16)
+        c_copy.append(go([remote(csend.at[i], crecv.at[i, m - 1], xp[m]) for m in (2, 1, 3)]))
+    arrived(wy)
+    a_own = wv.at[z, x, core, pl.ds(0, 32)]
+    b_own = wv.at[z, x, core, pl.ds(32, 32)]
+    w1a = go([remote(a_own, a_own, xp[m]) for m in (2, 1, 3)])
+    r_copy = []
+    for i in range(2):
+        arrived(c_copy[i])
+        rsend[i] = (
+            (cown[i] + crecv[i, 0].astype(F32)) + (crecv[i, 1].astype(F32) + crecv[i, 2].astype(F32))
+        ).astype(BF16)
+        r_copy.append(go([remote(rsend.at[i], rrecv.at[i, m - 1], zp[m]) for m in (2, 1, 3)]))
+    w1b = go([remote(b_own, b_own, zp[m]) for m in (2, 1, 3)])
+    x_copy = []
+    for i in range(2):
+        xfull[0, mine_h[i]] = crecv[i, 0].astype(F32)
+        xfull[1, mine_h[i]] = crecv[i, 1].astype(F32) + crecv[i, 2].astype(F32)
+        x12 = xfull.at[pl.ds(0, 2), mine_h[i]]
+        x_copy += go([remote(x12, x12, sib)])
+    for i in range(2):
+        arrived(r_copy[i])
+        xfull[2, mine_h[i]] = rrecv[i, 0].astype(F32)
+        xfull[3, mine_h[i]] = rrecv[i, 1].astype(F32) + rrecv[i, 2].astype(F32)
+        x34 = xfull.at[pl.ds(2, 2), mine_h[i]]
+        x_copy += go([remote(x34, x34, sib)])
+    w2a_src = wv.at[z, :, core, pl.ds(0, 32)]
     w2b_src = wv.at[:, x, core, pl.ds(32, 32)]
-    w2b = go([remote(w2b_src, w2b_src, xp[m]) for m in (1, 2, 3)])
-    arrived(r_copy)
-    xfull[2, half] = rrecv[0].astype(F32)
-    xfull[3, half] = rrecv[1].astype(F32) + rrecv[2].astype(F32)
-    x34 = xfull.at[pl.ds(2, 2), half]
-    x34_copy = go([remote(x34, x34, sib)])
-    w2a_src = wv.at[z, :, core, pl.ds(0, 32)]
-    w2a = go([remote(w2a_src, w2a_src, zp[m]) for m in (1, 2, 3)])
-    arrived(x12_copy)
-    arrived(x34_copy)
-    fwd = go([remote(s, s, sib) for s in (w2a_src, w2b_src)])
+    arrived(w1a)
+    w2a = go([remote(w2a_src, w2a_src, zp[m]) for m in (2, 1, 3)])
+    arrived(x_copy)
+    for i in range(2):
+        arrived(t_copy[2 + i])
     q_load.wait()
 
     bits = [core, lax.rem(x, 2), x // 2, lax.rem(z, 2), z // 2]
@@ -222,38 +229,47 @@
                 res.append((part[p // 2][(p % 2) * SPAN : (p % 2 + 1) * SPAN] + carried).astype(BF16))
             put(cols, rows, jnp.concatenate(res, axis=0))
 
-    att_copies = []
-    for j in range(4):
-        def to_send(cols, rows, value):
-            qv[rows, cols] = value
-
-        def keep(cols, rows, value, j=j):
-            att[y, pl.ds(j * GR, GR), cols] = value
-
-        batch = []
+    def att_copy(j, m):
+        g = partner(y, m) * 4 + j
+        return pltpu.make_async_remote_copy(
+            src_ref=qv.at[pl.ds(pl.multiple_of(g * GR, GR), GR)],
+            dst_ref=att.at[y, pl.ds(pl.multiple_of(j * GR, GR), GR)],
+            send_sem=att_send.at[j * 3 + m - 1], recv_sem=att_recv.at[j * 3 + m - 1],
+            device_id=yp[m], device_id_type=MESH,
+        )
+
+    def to_send(cols, rows, value):
+        qv[rows, cols] = value
+
+    def attention_round(j):
+        def keep(cols, rows, value):
+            att[y, pl.ds(pl.multiple_of(j * GR, GR), GR), cols] = value
+
         for m in (2, 1, 3):
-            g = partner(y, m) * 4 + j
-            attend(g, to_send)
-            batch += go([
-                remote(qv.at[pl.ds(pl.multiple_of(g * GR, GR), GR)], att.at[y, pl.ds(j * GR, GR)], yp[m])
-            ])
-        att_copies.append(batch)
+            attend(partner(y, m) * 4 + j, to_send)
+            att_copy(j, m).start()
         attend(y * 4 + j, keep)
 
-    arrived(w2a)
-    arrived(w2b)
-    for m in (1, 2, 3):
+    def attention_loop(j, carry):
+        attention_round(j)
+        return carry
+
+    lax.fori_loop(0, 1, attention_loop, 0)
+    arrived(w1b)
+    w2b = go([remote(w2b_src, w2b_src, xp[m]) for m in (2, 1, 3)])
+    fwd = go([remote(c, c, sib) for c in (w2a_src, w2b_src)])
+    lax.fori_loop(1, 4, attention_loop, 0)
+
+    for i, m in enumerate((2, 1, 3)):
+        arrived([w2a[i], w2b[i]])
         a = wv.at[partner(z, m), :, core, pl.ds(0, 32)]
         b = wv.at[:, partner(x, m), core, pl.ds(32, 32)]
         fwd += go([remote(a, a, sib), remote(b, b, sib)])
     arrived(fwd)
     g_load.wait()
 
-    stores = []
-    for j in range(4):
-        arrived(att_copies[j])
-
-        def normalize(i, carry, j=j):
+    def normalize(j):
+        def tile(i, carry):
             rows = pl.ds(pl.multiple_of(j * GR + i * 16, 16), 16)
             a = jnp.concatenate([att[s, rows, :] for s in range(4)], axis=1).astype(F32)
             gt = gv[rows, :].astype(F32)
@@ -264,40 +280,67 @@
             ).astype(BF16)
             return carry
 
-        lax.fori_loop(0, GR // 16, normalize, 0)
-        for n in range(4):
-            w = wv[n].reshape(512, 2048)
-            ov[pl.ds(j * GR, GR), n * 512 : (n + 1) * 512] = lax.dot_general(
-                nrm[...], w, NT, preferred_element_type=F32
-            ).astype(BF16)
-        st = local(ov.at[pl.ds(j * GR, GR)], out_hbm.at[pl.ds(j * GR, GR)])
-        st.start()
-        stores.append(st)
-
-    for st in stores:
-        st.wait()
+        lax.fori_loop(0, GR // 16, tile, 0)
+
+    def project_loop(j, carry):
+        for m in (1, 2, 3):
+            att_copy(j, m).wait_recv()
+        normalize(j)
+        project(nrm, wv, lambda cols, value: ov.__setitem__((pl.ds(pl.multiple_of(j * GR, GR), GR), cols), value))
+        return carry
+
+    lax.fori_loop(0, 3, project_loop, 0)
+    for m in (1, 2, 3):
+        att_copy(3, m).wait_recv()
+    normalize(3)
+
     for c in everything:
         c.wait_send()
+    for j in range(4):
+        for m in (1, 2, 3):
+            att_copy(j, m).wait_send()
+
+
+def project(nrm, wv, put):
+    for n in range(4):
+        value = lax.dot_general(nrm[...], wv[n].reshape(512, 2048), NT, preferred_element_type=F32)
+        put(slice(n * 512, (n + 1) * 512), value.astype(BF16))
+
+
+def last_kernel(ov, nrm, wv, out_hbm, tail, sem):
+    stores = [pltpu.make_async_copy(ov.at[pl.ds(j * GR, GR)], out_hbm.at[pl.ds(j * GR, GR)], sem.at[j]) for j in range(3)]
+    for c in stores:
+        c.start()
+
+    def put(cols, value):
+        tail[:, cols] = value
+
+    project(nrm, wv, put)
+    stores.append(pltpu.make_async_copy(tail, out_hbm.at[pl.ds(3 * GR, GR)], sem.at[3]))
+    stores[3].start()
+    for c in stores:
+        c.wait()
 
 
 def local_step(queries, keys, values, lam_index, level_weights, gate, norm_gain, out_weight):
     any_spec = pl.BlockSpec(memory_space=pl.ANY)
     smem = pl.BlockSpec(memory_space=pltpu.SMEM)
     vmem = pl.BlockSpec(memory_space=pltpu.VMEM)
-    return pl.pallas_call(
+    ov, nrm, wv = pl.pallas_call(
         kernel,
-        out_shape=jax.ShapeDtypeStruct((1024, 2048), BF16),
+        out_shape=[
+            pltpu.VMEM((3 * GR, 2048), BF16),
+            pltpu.VMEM((GR, 2048), BF16),
+            pltpu.VMEM((4, 4, 2, 64, 2048), BF16),
+        ],
         in_specs=[smem, smem, any_spec, any_spec, any_spec, any_spec, vmem, any_spec],
-        out_specs=any_spec,
+        out_specs=[vmem] * 3,
         scratch_shapes=[
             pltpu.VMEM((4096, 512), BF16),
             pltpu.VMEM((4096, 512), BF16),
             pltpu.VMEM((4096, 512), BF16),
             pltpu.VMEM((1024, 2048), BF16),
             pltpu.VMEM((4, 1024, 512), BF16),
-            pltpu.VMEM((4, 4, 2, 64, 2048), BF16),
-            pltpu.VMEM((1024, 2048), BF16),
-            pltpu.VMEM((GR, 2048), BF16),
             pltpu.VMEM((4, 16, DK, DK), F32),
             pltpu.VMEM((4, 8, DK, DK), F32),
             pltpu.VMEM((4, 4, DK, DK), F32),
@@ -306,21 +349,31 @@
             pltpu.VMEM((4, DK, DK), F32),
             pltpu.VMEM((2, DK, DK), F32),
             pltpu.VMEM((2, DK, DK), BF16),
-            pltpu.VMEM((3, 2, DK, DK), BF16),
+            pltpu.VMEM((2, 3, DK, DK), BF16),
             pltpu.VMEM((2, DK, DK), BF16),
-            pltpu.VMEM((3, 2, DK, DK), BF16),
+            pltpu.VMEM((2, 3, DK, DK), BF16),
             pltpu.VMEM((4, 4, DK, DK), F32),
             pltpu.SemaphoreType.DMA((16,)),
-            pltpu.SemaphoreType.DMA((48,)),
-            pltpu.SemaphoreType.DMA((48,)),
+            pltpu.SemaphoreType.DMA((64,)),
+            pltpu.SemaphoreType.DMA((64,)),
+            pltpu.SemaphoreType.DMA((12,)),
+            pltpu.SemaphoreType.DMA((12,)),
         ],
         compiler_params=pltpu.CompilerParams(
-            collective_id=0, has_side_effects=True, vmem_limit_bytes=58 * 1024 * 1024
+            collective_id=0, has_side_effects=True, vmem_limit_bytes=46 * 1024 * 1024
         ),
     )(
         lam_index, jnp.transpose(level_weights, (2, 1, 0)), queries, keys, values, gate,
         norm_gain.reshape(1, 2048), jnp.transpose(out_weight),
     )
+    return pl.pallas_call(
+        last_kernel,
+        out_shape=jax.ShapeDtypeStruct((1024, 2048), BF16),
+        in_specs=[vmem] * 3,
+        out_specs=any_spec,
+        scratch_shapes=[pltpu.VMEM((GR, 2048), BF16), pltpu.SemaphoreType.DMA((4,))],
+        compiler_params=pltpu.CompilerParams(vmem_limit_bytes=20 * 1024 * 1024),
+    )(ov, nrm, wv)
 
 
 def solution(mesh):

time: 89.9 us -> 80.7 us (0.90)
  local copies, waits for them, and re-layouts: 4.79 us -> 0 us
  Pallas kernels: 83.9 us -> 80 us
    unnamed x1 -> x0, local copies, waits for them, and re-layouts: 4.79 us -> none
    pallas_call x1 -> x2, Pallas kernels: 83.9 us -> 80 us  [the longest x1 76.6 us: local_step(): pl.pallas_call(kernel, out_shape=[pltpu.VMEM((3 * GR, 2048), BF16), pltpu...]
where the time goes in v2:
time: 80.7 us; the launch traced here: 80.2 us
  Pallas kernels  80 us (99%)
    pallas_call x1, Pallas kernels, local_step(): pl.pallas_call(kernel, out_shape=[pltpu.VMEM((3 * GR, 2048), BF16), pltpu...  76.6 us
    pallas_call x1, Pallas kernels, local_step(): pl.pallas_call(last_kernel, out_shape=jax.ShapeDtypeStruct((1024, 2048),...  3.37 us

profile of v2, /device:TPU:0, one launch (start us, length us, event | category | flops | bytes accessed | tf_op | source)
XLA Modules:
  0.0 80.2 jit_solution(151315725505308276)
XLA Ops:
  0.0 76.6 %shard_map.82 = (bf16[768,2048]{1,0:T(8,128)(2,1)S(1)}, bf16[256,2048]{1,0:T(8,128)(2,1)S(1)}, bf16[4,4,2,64,2048]{4,3,2,1,0:T(8,128)(2,1)S(1)}) custom-call(s32[64]{0:T(128)} %lam.1, f32[12,4,16]{2,1,0:T(4,128)} %bitcast.4, bf16[4096,512]{1,0:T(8,128)(2,1)} %q_hbm.1, bf16[4096,512]{1,0:T(8,128)(2,1)} %k_hbm.1, bf16[4096,512]{1,0:T(8,128)(2,1)} %v_hbm.1, ...), custom_call_target="tpu_custom_call" | custom-call | tf_op jit(solution)/shard_map/pallas_call | solution.py:329
  76.6 3.4 %shard_map.83 = bf16[1024,2048]{1,0:T(8,128)(2,1)} custom-call(bf16[768,2048]{1,0:T(8,128)(2,1)S(1)} %get-tuple-element.8.ov, bf16[256,2048]{1,0:T(8,128)(2,1)S(1)} %get-tuple-element.9.nrm, bf16[4,4,2,64,2048]{4,3,2,1,0:T(8,128)(2,1)S(1)} %get-tuple-element.10.wv), custom_call_target="tpu_custom_call" | custom-call | tf_op jit(solution)/shard_map/pallas_call | solution.py:369

commit v3 on v2

--- a/solution.py
+++ b/solution.py
@@ -14,6 +14,8 @@
 GR = GROUP * SPAN
 SCALE = [2.0 ** (-0.5 * l) * DK**-0.5 for l in range(LEVELS)]
 MESH = pl.DeviceIdType.MESH
+LAST = 3
+TAIL = GR
 F32 = jnp.float32
 UNROLL = True
 BF16 = jnp.bfloat16
@@ -87,13 +89,12 @@
     for c in range(4):
         rows = pl.ds(c * 1024, 1024)
         pair = (local(k_hbm.at[rows], kv.at[rows]), local(v_hbm.at[rows], vv.at[rows]))
+        kv_loads.append(pair)
+    for pair in kv_loads[:2]:
         for cp in pair:
             cp.start()
-        kv_loads.append(pair)
     q_load = local(q_hbm, qv)
-    q_load.start()
     g_load = local(gate_hbm, gv)
-    g_load.start()
 
     barrier = pltpu.get_barrier_semaphore()
     friends = [sib] + [d[m] for d in (xp, zp, yp) for m in (1, 2, 3)]
@@ -103,6 +104,8 @@
     for c in range(4):
         for cp in kv_loads[c]:
             cp.wait()
+        for cp in kv_loads[c + 2] if c < 2 else [q_load] if c == 3 else []:
+            cp.start()
 
         def states(i, carry):
             g = c * 4 + i
@@ -124,9 +127,10 @@
 
     w_load.wait()
     pl.semaphore_wait(barrier, len(friends))
-    mine_h = [2 * core, 2 * core + 1]
-    sib_h = [2 * (1 - core), 2 * (1 - core) + 1]
+    mine_h = [core, 2 + core]
+    sib_h = [1 - core, 3 - core]
     t_copy = [go([remote(tot.at[h], tsib.at[h], sib)]) for h in sib_h]
+    g_load.start()
     mine = wv.at[z, x, core, pl.ds(pl.multiple_of(y * 16, 16), 16)]
     wy = go([remote(mine, mine, yp[m]) for m in (1, 2, 3)])
     t_copy += [go([remote(tot.at[h], tsib.at[h], sib)]) for h in mine_h]
@@ -153,20 +157,17 @@
         xfull[0, mine_h[i]] = crecv[i, 0].astype(F32)
         xfull[1, mine_h[i]] = crecv[i, 1].astype(F32) + crecv[i, 2].astype(F32)
         x12 = xfull.at[pl.ds(0, 2), mine_h[i]]
-        x_copy += go([remote(x12, x12, sib)])
+        x_copy.append(go([remote(x12, x12, sib)]))
+    w2a_src = wv.at[z, :, core, pl.ds(0, 32)]
+    w2b_src = wv.at[:, x, core, pl.ds(32, 32)]
     for i in range(2):
         arrived(r_copy[i])
         xfull[2, mine_h[i]] = rrecv[i, 0].astype(F32)
         xfull[3, mine_h[i]] = rrecv[i, 1].astype(F32) + rrecv[i, 2].astype(F32)
         x34 = xfull.at[pl.ds(2, 2), mine_h[i]]
-        x_copy += go([remote(x34, x34, sib)])
-    w2a_src = wv.at[z, :, core, pl.ds(0, 32)]
-    w2b_src = wv.at[:, x, core, pl.ds(32, 32)]
+        x_copy[i] += go([remote(x34, x34, sib)])
     arrived(w1a)
     w2a = go([remote(w2a_src, w2a_src, zp[m]) for m in (2, 1, 3)])
-    arrived(x_copy)
-    for i in range(2):
-        arrived(t_copy[2 + i])
     q_load.wait()
 
     bits = [core, lax.rem(x, 2), x // 2, lax.rem(z, 2), z // 2]
@@ -177,12 +178,12 @@
     high = lane <= row + SPAN
     left = lane < SPAN
 
-    def attend(g, put):
+    def attend(g, pair, put):
         rows = pl.ds(pl.multiple_of(g * GR, GR), GR)
         g2, g4, g8 = g // 2, g // 4, g // 8
         own_bit = [lax.rem(b, 2).astype(F32) for b in (g, g2, g4, g8)]
         s1, s2, s4, s8 = flip(g), flip(g2), flip(g4), flip(g8)
-        for h in range(4):
+        for h in (2 * pair, 2 * pair + 1):
             cols = slice(h * DK, (h + 1) * DK)
             qg, kg, vg = qv[rows, cols], kv[rows, cols], vv[rows, cols]
             s = lax.dot_general(qg, kg, NT, preferred_element_type=F32)
@@ -229,76 +230,110 @@
                 res.append((part[p // 2][(p % 2) * SPAN : (p % 2 + 1) * SPAN] + carried).astype(BF16))
             put(cols, rows, jnp.concatenate(res, axis=0))
 
-    def att_copy(j, m):
+    def att_copy(j, m, part):
         g = partner(y, m) * 4 + j
+        if j is LAST:
+            cols, rows, skip = pl.ds(0, 512), GR // 2, part * (GR // 2)
+        else:
+            cols, rows, skip = pl.ds(part * 256, 256), GR, 0
         return pltpu.make_async_remote_copy(
-            src_ref=qv.at[pl.ds(pl.multiple_of(g * GR, GR), GR)],
-            dst_ref=att.at[y, pl.ds(pl.multiple_of(j * GR, GR), GR)],
-            send_sem=att_send.at[j * 3 + m - 1], recv_sem=att_recv.at[j * 3 + m - 1],
+            src_ref=qv.at[pl.ds(pl.multiple_of(g * GR + skip, 128), rows), cols],
+            dst_ref=att.at[y, pl.ds(pl.multiple_of(j * GR + skip, 128), rows), cols],
+            send_sem=att_send.at[j * 6 + part * 3 + m - 1], recv_sem=att_recv.at[j * 6 + part * 3 + m - 1],
             device_id=yp[m], device_id_type=MESH,
         )
 
     def to_send(cols, rows, value):
         qv[rows, cols] = value
 
-    def attention_round(j):
+    def attention_round(j, ready=None):
         def keep(cols, rows, value):
             att[y, pl.ds(pl.multiple_of(j * GR, GR), GR), cols] = value
 
-        for m in (2, 1, 3):
-            attend(partner(y, m) * 4 + j, to_send)
-            att_copy(j, m).start()
-        attend(y * 4 + j, keep)
+        for part in range(2):
+            if ready is not None:
+                ready(part)
+            for m in (2, 1, 3):
+                attend(partner(y, m) * 4 + j, part, to_send)
+                if j is not LAST:
+                    att_copy(j, m, part).start()
+        if j is LAST:
+            for part in range(2):
+                for m in (2, 1, 3):
+                    att_copy(j, m, part).start()
+        for part in range(2):
+            attend(y * 4 + j, part, keep)
 
     def attention_loop(j, carry):
         attention_round(j)
         return carry
 
-    lax.fori_loop(0, 1, attention_loop, 0)
+    def ready(part):
+        arrived(x_copy[part])
+        arrived(t_copy[2 + part])
+
+    attention_round(0, ready)
     arrived(w1b)
     w2b = go([remote(w2b_src, w2b_src, xp[m]) for m in (2, 1, 3)])
     fwd = go([remote(c, c, sib) for c in (w2a_src, w2b_src)])
-    lax.fori_loop(1, 4, attention_loop, 0)
-
+    lax.fori_loop(1, 3, attention_loop, 0)
+    attention_round(LAST)
+
+    def normalize(first, count):
+        def tile(i, carry):
+            rows = pl.ds(pl.multiple_of(first + i * 16, 16), 16)
+            a = jnp.concatenate([att[s, rows, :] for s in range(4)], axis=1).astype(F32)
+            gt = gv[rows, :].astype(F32)
+            gated = a * (gt * (0.5 + 0.5 * jnp.tanh(0.5 * gt)))
+            mean = jnp.mean(gated * gated, axis=1, keepdims=True)
+            nrm[rows, :] = (gated * lax.rsqrt(mean + 1e-6) * gain[...]).astype(BF16)
+            return carry
+
+        lax.fori_loop(0, count // 16, tile, 0, unroll=2)
+
+    def chunk(first, count):
+        rows = pl.ds(pl.multiple_of(first, count), count)
+
+        def put(cols, value):
+            ov[rows, cols] = value
+
+        project(nrm.at[rows], wv, put)
+
+    def regrouped(j, parts=(0, 1)):
+        for part in parts:
+            for m in (1, 2, 3):
+                att_copy(j, m, part).wait_recv()
+
+    def project_loop(j, carry):
+        chunk(j * GR, GR)
+        return carry
+
+    g_load.wait()
+    regrouped(0)
+    normalize(0, GR)
     for i, m in enumerate((2, 1, 3)):
         arrived([w2a[i], w2b[i]])
         a = wv.at[partner(z, m), :, core, pl.ds(0, 32)]
         b = wv.at[:, partner(x, m), core, pl.ds(32, 32)]
         fwd += go([remote(a, a, sib), remote(b, b, sib)])
+    regrouped(1)
+    normalize(GR, GR)
     arrived(fwd)
-    g_load.wait()
-
-    def normalize(j):
-        def tile(i, carry):
-            rows = pl.ds(pl.multiple_of(j * GR + i * 16, 16), 16)
-            a = jnp.concatenate([att[s, rows, :] for s in range(4)], axis=1).astype(F32)
-            gt = gv[rows, :].astype(F32)
-            gated = a * (gt / (1.0 + jnp.exp(-gt)))
-            mean = jnp.mean(gated * gated, axis=1, keepdims=True)
-            nrm[pl.ds(pl.multiple_of(i * 16, 16), 16), :] = (
-                gated * lax.rsqrt(mean + 1e-6) * gain[...]
-            ).astype(BF16)
-            return carry
-
-        lax.fori_loop(0, GR // 16, tile, 0)
-
-    def project_loop(j, carry):
-        for m in (1, 2, 3):
-            att_copy(j, m).wait_recv()
-        normalize(j)
-        project(nrm, wv, lambda cols, value: ov.__setitem__((pl.ds(pl.multiple_of(j * GR, GR), GR), cols), value))
-        return carry
-
-    lax.fori_loop(0, 3, project_loop, 0)
-    for m in (1, 2, 3):
-        att_copy(3, m).wait_recv()
-    normalize(3)
+    lax.fori_loop(0, 2, project_loop, 0)
+    regrouped(2)
+    normalize(2 * GR, GR)
+    lax.fori_loop(2, 3, project_loop, 0)
+    regrouped(LAST, (0,))
+    normalize(3 * GR, GR // 2)
+    regrouped(LAST, (1,))
+    normalize(3 * GR + GR // 2, GR // 2)
 
     for c in everything:
         c.wait_send()
     for j in range(4):
-        for m in (1, 2, 3):
-            att_copy(j, m).wait_send()
+        for part in range(2):
+            for m in (1, 2, 3):
+                att_copy(LAST if j == 3 else j, m, part).wait_send()
 
 
 def project(nrm, wv, put):
@@ -308,17 +343,16 @@
 
 
 def last_kernel(ov, nrm, wv, out_hbm, tail, sem):
-    stores = [pltpu.make_async_copy(ov.at[pl.ds(j * GR, GR)], out_hbm.at[pl.ds(j * GR, GR)], sem.at[j]) for j in range(3)]
-    for c in stores:
-        c.start()
-
-    def put(cols, value):
-        tail[:, cols] = value
-
-    project(nrm, wv, put)
-    stores.append(pltpu.make_async_copy(tail, out_hbm.at[pl.ds(3 * GR, GR)], sem.at[3]))
-    stores[3].start()
-    for c in stores:
+    done = pltpu.make_async_copy(ov, out_hbm.at[pl.ds(0, 1024 - TAIL)], sem.at[0])
+    done.start()
+    stores = []
+    for n in range(4):
+        cols = slice(n * 512, (n + 1) * 512)
+        value = lax.dot_general(nrm[1024 - TAIL :], wv[n].reshape(512, 2048), NT, preferred_element_type=F32)
+        tail[:, cols] = value.astype(BF16)
+        stores.append(pltpu.make_async_copy(tail.at[:, cols], out_hbm.at[pl.ds(1024 - TAIL, TAIL), cols], sem.at[1 + n]))
+        stores[-1].start()
+    for c in [done] + stores:
         c.wait()
 
 
@@ -329,8 +363,8 @@
     ov, nrm, wv = pl.pallas_call(
         kernel,
         out_shape=[
-            pltpu.VMEM((3 * GR, 2048), BF16),
-            pltpu.VMEM((GR, 2048), BF16),
+            pltpu.VMEM((1024 - TAIL, 2048), BF16),
+            pltpu.VMEM((1024, 2048), BF16),
             pltpu.VMEM((4, 4, 2, 64, 2048), BF16),
         ],
         in_specs=[smem, smem, any_spec, any_spec, any_spec, any_spec, vmem, any_spec],
@@ -356,8 +390,8 @@
             pltpu.SemaphoreType.DMA((16,)),
             pltpu.SemaphoreType.DMA((64,)),
             pltpu.SemaphoreType.DMA((64,)),
-            pltpu.SemaphoreType.DMA((12,)),
-            pltpu.SemaphoreType.DMA((12,)),
+            pltpu.SemaphoreType.DMA((24,)),
+            pltpu.SemaphoreType.DMA((24,)),
         ],
         compiler_params=pltpu.CompilerParams(
             collective_id=0, has_side_effects=True, vmem_limit_bytes=46 * 1024 * 1024
@@ -371,7 +405,7 @@
         out_shape=jax.ShapeDtypeStruct((1024, 2048), BF16),
         in_specs=[vmem] * 3,
         out_specs=any_spec,
-        scratch_shapes=[pltpu.VMEM((GR, 2048), BF16), pltpu.SemaphoreType.DMA((4,))],
+        scratch_shapes=[pltpu.VMEM((TAIL, 2048), BF16), pltpu.SemaphoreType.DMA((5,))],
         compiler_params=pltpu.CompilerParams(vmem_limit_bytes=20 * 1024 * 1024),
     )(ov, nrm, wv)
 

time: 80.7 us -> 76 us (0.942)
  Pallas kernels: 80 us -> 75.7 us
    pallas_call x1, Pallas kernels: 76.6 us -> 72.5 us  [local_step(): pl.pallas_call(kernel, out_shape=[pltpu.VMEM((1024 - TAIL, 2048), BF16),...]
where the time goes in v3:
time: 76 us; the launch traced here: 75.8 us
  Pallas kernels  75.7 us (100%)
    pallas_call x1, Pallas kernels, local_step(): pl.pallas_call(kernel, out_shape=[pltpu.VMEM((1024 - TAIL, 2048), BF16),...  72.5 us
    pallas_call x1, Pallas kernels, local_step(): pl.pallas_call(last_kernel, out_shape=jax.ShapeDtypeStruct((1024, 2048),...  3.11 us

profile of v3, /device:TPU:0, one launch (start us, length us, event | category | flops | bytes accessed | tf_op | source)
XLA Modules:
  0.0 75.8 jit_solution(15945851601305185988)
XLA Ops:
  0.0 72.5 %shard_map.82 = (bf16[768,2048]{1,0:T(8,128)(2,1)S(1)}, bf16[1024,2048]{1,0:T(8,128)(2,1)S(1)}, bf16[4,4,2,64,2048]{4,3,2,1,0:T(8,128)(2,1)S(1)}) custom-call(s32[64]{0:T(128)} %lam.1, f32[12,4,16]{2,1,0:T(4,128)} %bitcast.4, bf16[4096,512]{1,0:T(8,128)(2,1)} %q_hbm.1, bf16[4096,512]{1,0:T(8,128)(2,1)} %k_hbm.1, bf16[4096,512]{1,0:T(8,128)(2,1)} %v_hbm.1, ...), custom_call_target="tpu_custom_call" | custom-call | tf_op jit(solution)/shard_map/pallas_call | solution.py:363
  72.6 3.1 %shard_map.83 = bf16[1024,2048]{1,0:T(8,128)(2,1)} custom-call(bf16[768,2048]{1,0:T(8,128)(2,1)S(1)} %get-tuple-element.8.ov, bf16[1024,2048]{1,0:T(8,128)(2,1)S(1)} %get-tuple-element.9.nrm, bf16[4,4,2,64,2048]{4,3,2,1,0:T(8,128)(2,1)S(1)} %get-tuple-element.10.wv), custom_call_target="tpu_custom_call" | custom-call | tf_op jit(solution)/shard_map/pallas_call | solution.py:403
